TPU v7x, 32 devices: a whole 2x2x4 slice. The times are simulated.
32 devices in a mesh: groups: 2 (over y), etp: 4 (over x, core), expert: 4 (over z).
Axes of the slice: x: 2, y: 2, z: 4, core: 2. Of those that a mesh axis runs over, the one named last changes fastest.
Arguments:
- tokens: bfloat16 [1024, 3072], P(('groups', 'expert')), parts along dimension 0, may hold values from -6 to 6
- expert_ids: int32 [1024, 2], P(('groups', 'expert')), parts along dimension 0, may hold values from 0 to 3, as said below
- route_weights: float32 [1024, 2], P(('groups', 'expert')), parts along dimension 0, may hold values from 0.1 to 1
- w_gate: bfloat16 [4, 3072, 8192], P('expert', None, 'etp'), may hold values from -0.109375 to 0.109375
- w_up: bfloat16 [4, 3072, 8192], P('expert', None, 'etp'), may hold values from -0.109375 to 0.109375
- w_down: bfloat16 [4, 8192, 3072], P('expert', 'etp'), may hold values from -0.09375 to 0.09375
Outputs:
- layer_out: bfloat16 [1024, 3072], P(('groups', 'expert'), 'etp'), parts along dimension 0
There are 2 independent parts, one for each index of `groups`. A program takes and returns all parts, laid end to end along the dimension named above; an argument that names none is the same for every part. Nothing has to cross between parts.
Inputs may be any that keep to these rules, and one draw needn't show every extreme that they name: `expert_ids`: the two experts of a token differ. In each aligned block of 128 rows no expert is named by more than 80 rows, and one expert, the same in all blocks of a part, is named by exactly 80 rows in every block.
All inputs are finite; a program needn't handle non-finite values.
Results may differ from a plain program's by a relative error of at most 0.01.
Values may be sent and summed in bfloat16 or wider, within the bound.
A program may use at most 128 MiB of HBM per device.

v0:
```python
import jax
import jax.numpy as jnp
from jax import lax
from jax.sharding import PartitionSpec as P


def route_places(expert_ids, experts, capacity):
    routes_flat = expert_ids.reshape(-1)
    labels = jnp.arange(experts, dtype=jnp.int32)
    matches = (routes_flat[:, None] == labels[None, :]).astype(jnp.int32)
    earlier = jnp.cumsum(matches, axis=0) - matches
    slots = jnp.sum(earlier * matches, axis=1)
    return routes_flat * capacity + slots


def dispatch_rows(source_rows, places, experts, capacity):
    count_rows = source_rows.shape[0]
    targets = jnp.arange(experts * capacity, dtype=jnp.int32)
    matrix = (targets[:, None] == places[None, :]).astype(jnp.bfloat16)
    matrix = matrix.reshape(experts * capacity, count_rows, 2).sum(axis=2)
    placed = jnp.dot(matrix, source_rows, preferred_element_type=jnp.float32).astype(jnp.bfloat16)
    return placed.reshape(experts, capacity, source_rows.shape[1])


def swiglu(gate_act, up_act):
    return (jax.nn.silu(gate_act) * up_act).astype(jnp.bfloat16)


def body(tokens, expert_ids, route_weights, w_gate, w_up, w_down):
    experts = lax.axis_size("expert")
    shards = lax.axis_size("etp")
    tok_rows = tokens.shape[0]
    capacity = tok_rows * 5 // 8
    model_width = tokens.shape[1]
    slice_width = model_width // shards
    places = route_places(expert_ids, experts, capacity)
    gate_local = w_gate[0]
    up_local = w_up[0]
    down_local = w_down[0]
    outgoing = dispatch_rows(tokens, places, experts, capacity)
    arrived = lax.all_to_all(outgoing, "expert", split_axis=0, concat_axis=0, tiled=True)
    sources = arrived.shape[0]
    items = arrived.shape[1]
    rows_in = arrived.reshape(sources * items, model_width)
    gate_act = jnp.dot(rows_in, gate_local, preferred_element_type=jnp.float32)
    up_act = jnp.dot(rows_in, up_local, preferred_element_type=jnp.float32)
    hidden = swiglu(gate_act, up_act)
    partial_rows = jnp.dot(hidden, down_local, preferred_element_type=jnp.float32).astype(
        jnp.bfloat16
    )
    partial_value = partial_rows.reshape(sources, items, model_width)
    summed = lax.psum_scatter(partial_value, "etp", scatter_dimension=2, tiled=True).astype(
        jnp.float32
    )
    expert_out = summed.astype(jnp.bfloat16)
    returned = lax.all_to_all(expert_out, "expert", split_axis=0, concat_axis=0, tiled=True)
    picked = returned.reshape(experts * capacity, slice_width)[places]
    weighted = picked.astype(jnp.float32) * route_weights.reshape(-1)[:, None]
    combined = jnp.sum(weighted.reshape(tok_rows, 2, slice_width), axis=1)
    return combined.astype(jnp.bfloat16)


def solution(mesh):
    placed = (
        P(("groups", "expert"), None),
        P(("groups", "expert"), None),
        P(("groups", "expert"), None),
        P("expert", None, "etp"),
        P("expert", None, "etp"),
        P("expert", "etp", None),
    )
    return jax.shard_map(
        body, mesh=mesh, in_specs=placed, out_specs=P(("groups", "expert"), "etp"), check_vma=False
    )
```

profile of v0, /device:TPU:0, one launch (start us, length us, event | category | flops | bytes accessed | tf_op | source)
XLA Modules:
  0.0 147.8 jit_solution(228023872763263080)
XLA Ops:
  6.5 0.9 copy.17
  7.4 0.1 eq.44
  7.5 0.1 eq.40
  7.7 1.2 reduce-window.6
  8.9 0.1 slice.10
  9.0 0.1 copy.20
  9.1 0.1 copy.21
  9.2 0.1 add_bitcast_fusion
  9.3 0.1 reduce_sum.35
  9.5 0.1 copy.22
  9.6 0.1 fusion.18
  9.6 0.7 convolution_convert_fusion
  10.3 51.5 %all_to_all.10 = bf16[4,80,3072]{2,1,0:T(8,128)(2,1)S(1)} all-to-all(bf16[4,80,3072]{2,1,0:T(8,128)(2,1)S(1)} %bitcast.47), channel_id=1, replica_groups=mesh['groups'=2,'etp'=4,'expert'=4] {'expert'}, dimensions={0} | all-to-all | bytes 3932160 | tf_op jit(solution)/shard_map/all_to_all | solution.py:41
  61.8 8.8 %fusion.4 = f32[320,2048]{1,0:T(8,128)} fusion(bf16[320,3072]{1,0:T(8,128)(2,1)S(1)} %bitcast.49, bf16[1,3072,2048]{2,1,0:T(8,128)(2,1)} %param.9), kind=kOutput, calls=%fused_computation.5 | convolution fusion | flops 4026531840 | bytes 17170432 | tf_op jit(solution)/shard_map/dot_general | solution.py:45
  70.6 18.7 %fusion.6 = bf16[320,3072]{1,0:T(8,128)(2,1)} fusion(bf16[1,2048,3072]{2,1,0:T(8,128)(2,1)} %param.11, bf16[320,3072]{1,0:T(8,128)(2,1)S(1)} %bitcast.50, bf16[1,3072,2048]{2,1,0:T(8,128)(2,1)} %param.10, f32[320,2048]{1,0:T(8,128)} %fusion.4), kind=kOutput, calls=%fused_computation.8 | convolution fusion | flops 8057978880 | bytes 31719424 | tf_op jit(solution)/shard_map/dot_general | solution.py:48
  89.3 0.0 reduce-scatter.2.cloned.1.call-update
  89.3 29.9 %reduce-scatter.2.cloned.1.call-done = bf16[4,80,768]{2,1,0:T(8,128)(2,1)} async-done(((bf16[4,80,3072]{2,1,0:T(8,128)(2,1)}), bf16[4,80,768]{2,1,0:T(8,128)(2,1)}) %reduce-scatter.2.cloned.1.call-update) | async-done | bytes 491536 | tf_op jit(solution)/shard_map/reduce_scatter | solution.py:52
  119.3 4.6 %all-to-all-start.1 = ((bf16[4,80,768]{2,1,0:T(8,128)(2,1)}), bf16[4,80,768]{2,1,0:T(8,128)(2,1)S(1)}, u32[]{:S(2)}, u32[]{:S(2)}) async-start(bf16[4,80,768]{2,1,0:T(8,128)(2,1)} %reduce-scatter.2.cloned.1.call-done), calls=%async_computation.2 | async-start | bytes 983040 | tf_op jit(solution)/shard_map/all_to_all | solution.py:56
  123.9 0.1 mul.44
  124.0 0.1 copy.23
  124.2 13.5 %all-to-all-done.1 = bf16[4,80,768]{2,1,0:T(8,128)(2,1)S(1)} async-done(((bf16[4,80,768]{2,1,0:T(8,128)(2,1)}), bf16[4,80,768]{2,1,0:T(8,128)(2,1)S(1)}, u32[]{:S(2)}, u32[]{:S(2)}) %all-to-all-start.1) | async-done | bytes 491552 | tf_op jit(solution)/shard_map/all_to_all | solution.py:56
  137.7 1.2 gather_fusion
  138.9 0.4 reshape.90
  139.3 1.7 %multiply_reduce_fusion = bf16[128,768]{1,0:T(8,128)(2,1)} fusion(f32[128,2,768]{2,1,0:T(2,128)S(1)} %reshape.90, f32[128,2]{1,0:T(8,128)S(1)} %copy.23), kind=kLoop, calls=%fused_computation.11 | loop fusion | flops 294912 | bytes 984064 | tf_op jit(solution)/shard_map/reduce_sum | solution.py:59
  (12 shorter events, 0.1 us)
Async XLA Ops:
  6.5 3.1 %copy-start = (bf16[128,3072]{1,0:T(8,128)(2,1)S(1)}, bf16[128,3072]{1,0:T(8,128)(2,1)}, u32[]{:S(2)}) copy-start(bf16[128,3072]{1,0:T(8,128)(2,1)} %param.6) | copy-start | bytes 2359300
  6.5 112.7 %reduce-scatter.2.cloned.1.call-start = ((), (), s32[]{:S(2)}) async-start(), calls=%async_computation.3 | async-start | bytes 2457600 | tf_op jit(solution)/shard_map/reduce_scatter | solution.py:52
  89.3 34.7 %copy-start.1 = (f32[128,2]{0,1:T(2,128)S(1)}, f32[128,2]{0,1:T(2,128)}, u32[]{:S(2)}) copy-start(f32[128,2]{0,1:T(2,128)} %param.8) | copy-start | bytes 3076
  119.3 18.4 %all-to-all-start.1 = ((bf16[4,80,768]{2,1,0:T(8,128)(2,1)}), bf16[4,80,768]{2,1,0:T(8,128)(2,1)S(1)}, u32[]{:S(2)}, u32[]{:S(2)}) async-start(bf16[4,80,768]{2,1,0:T(8,128)(2,1)} %reduce-scatter.2.cloned.1.call-done), calls=%async_computation.2 | async-start | bytes 983040 | tf_op jit(solution)/shard_map/all_to_all | solution.py:56
Sparse Core Ops, SparseCore 0:
  89.5 29.7 reduce-scatter.1
where the time goes:
time: 148 us
  blocking collectives  51.5 us (35%)
  waiting for transfers between devices  43.5 us (29%)
  matrix products  28.2 us (19%)
  between operations  13.5 us (9%)
  starting transfers between devices  4.62 us (3%)
  local copies, waits for them, and re-layouts  3.44 us (2%)
  other arithmetic  3.14 us (2%)
    all_to_all x1, blocking collectives, body(): lax.all_to_all(outgoing, 'expert', split_axis=0, concat_axis=0, tiled=True)  51.5 us
    reduce_scatter x1, waiting for transfers between devices, body(): lax.psum_scatter(partial_value, 'etp', scatter_dimension=2, tiled=True)  29.9 us
    dot_general x1, matrix products, body(): jnp.dot(hidden, down_local, preferred_element_type=jnp.float32)  18.7 us
    all_to_all x1, waiting for transfers between devices, body(): lax.all_to_all(expert_out, 'expert', split_axis=0, concat_axis=0, tiled=T...  13.5 us
    dot_general x1, matrix products, body(): gate_act = jnp.dot(rows_in, gate_local, preferred_element_type=jnp.float32)  8.76 us
    all_to_all x1, starting transfers between devices, body(): lax.all_to_all(expert_out, 'expert', split_axis=0, concat_axis=0, tiled=T...  4.62 us
  transfers between devices with their start and end apart: 2, of which 2 were waited for; matrix products, arithmetic and copies ran while one was open for 0% of the time, Pallas kernels for 0%

commit v1 on v0

v1 whole, which is shorter than its diff:
```python
import functools

import jax
import jax.numpy as jnp
from jax import lax
from jax.experimental import pallas as pl
from jax.experimental.pallas import tpu as pltpu
from jax.sharding import PartitionSpec as P

MESH = pl.DeviceIdType.MESH
F32 = jnp.float32
BF16 = jnp.bfloat16
TILE = 256
PARTS = 4


def route_places(expert_ids, experts, capacity):
    routes_flat = expert_ids.reshape(-1)
    labels = jnp.arange(experts, dtype=jnp.int32)
    matches = (routes_flat[:, None] == labels[None, :]).astype(jnp.int32)
    earlier = jnp.cumsum(matches, axis=0) - matches
    slots = jnp.sum(earlier * matches, axis=1)
    return routes_flat * capacity + slots


def dispatch_rows(source_rows, places, experts, capacity):
    count_rows = source_rows.shape[0]
    targets = jnp.arange(experts * capacity, dtype=jnp.int32)
    matrix = (targets[:, None] == places[None, :]).astype(BF16)
    matrix = matrix.reshape(experts * capacity, count_rows, 2).sum(axis=2)
    placed = jnp.dot(matrix, source_rows, preferred_element_type=F32).astype(BF16)
    return placed.reshape(experts, capacity, source_rows.shape[1])


def wide_body(tokens, expert_ids, route_weights, w_gate, w_up, w_down):
    experts = lax.axis_size("expert")
    shards = lax.axis_size("etp")
    tok_rows = tokens.shape[0]
    capacity = tok_rows * 5 // 8
    model_width = tokens.shape[1]
    slice_width = model_width // shards
    places = route_places(expert_ids, experts, capacity)
    outgoing = dispatch_rows(tokens, places, experts, capacity)
    arrived = lax.all_to_all(outgoing, "expert", split_axis=0, concat_axis=0, tiled=True)
    rows_in = arrived.reshape(experts * capacity, model_width)
    gate_act = jnp.dot(rows_in, w_gate[0], preferred_element_type=F32)
    up_act = jnp.dot(rows_in, w_up[0], preferred_element_type=F32)
    hidden = (jax.nn.silu(gate_act) * up_act).astype(BF16)
    partial_rows = jnp.dot(hidden, w_down[0], preferred_element_type=F32).astype(BF16)
    partial_value = partial_rows.reshape(experts, capacity, model_width)
    expert_out = lax.psum_scatter(partial_value, "etp", scatter_dimension=2, tiled=True)
    returned = lax.all_to_all(expert_out, "expert", split_axis=0, concat_axis=0, tiled=True)
    picked = returned.reshape(experts * capacity, slice_width)[places]
    weighted = picked.astype(F32) * route_weights.reshape(-1)[:, None]
    combined = jnp.sum(weighted.reshape(tok_rows, 2, slice_width), axis=1)
    return combined.astype(BF16)


def layer_kernel(
    experts,
    ids_ref, wts_ref, tok_ref, gate_hbm, up_hbm, down_hbm,
    out_ref,
    gate, up, down, rows, outgoing, hidden, mix,
    core_out, core_in, far_sum, own_sum, x_out, x_in, z_out, returned,
    w_sem, z_send, z_recv, c_send, c_recv, x_send, x_recv, d_send, d_recv,
    pc_send, pc_recv, px_send, px_recv, pz_send, pz_recv,
):
    me = lax.axis_index("etp")
    z = lax.axis_index("expert")
    chip = me // 2
    core = me - chip * 2
    core_peer = chip * 2 + (1 - core)
    x_peer = (1 - chip) * 2 + core
    diagonal = (1 - chip) * 2 + (1 - core)
    tok_rows = tok_ref.shape[0]
    cap = rows.shape[2]
    width = rows.shape[3]
    total = experts * cap
    units = hidden.shape[1]

    in_chunk = gate.shape[0] // PARTS
    down_chunk = down.shape[0] // PARTS
    weight_copies = []
    for part in range(PARTS):
        at = slice(part * in_chunk, (part + 1) * in_chunk)
        weight_copies.append(pltpu.make_async_copy(gate_hbm.at[0, at], gate.at[at], w_sem.at[0, part]))
        weight_copies.append(pltpu.make_async_copy(up_hbm.at[0, at], up.at[at], w_sem.at[1, part]))
    for part in range(PARTS):
        at = slice(part * down_chunk, (part + 1) * down_chunk)
        weight_copies.append(pltpu.make_async_copy(down_hbm.at[0, at], down.at[at], w_sem.at[2, part]))
    for copy in weight_copies:
        copy.start()

    barrier = pltpu.get_barrier_semaphore()
    others = [lax.rem(z + d, experts) for d in range(experts)]
    for d in range(1, experts):
        pl.semaphore_signal(barrier, inc=1, device_id={"expert": others[d]}, device_id_type=MESH)
    for peer in (core_peer, x_peer):
        pl.semaphore_signal(barrier, inc=1, device_id={"etp": peer}, device_id_type=MESH)

    ids = ids_ref[...]
    lane = lax.broadcasted_iota(jnp.int32, (tok_rows, 128), 1)
    match = [ids[:, k : k + 1] == lane for k in range(2)]
    counts = (match[0].astype(F32) + match[1].astype(F32)).astype(BF16)
    row_at = lax.broadcasted_iota(jnp.int32, (tok_rows, tok_rows), 0)
    col_at = lax.broadcasted_iota(jnp.int32, (tok_rows, tok_rows), 1)
    before = (col_at < row_at).astype(F32).astype(BF16)
    earlier = jnp.dot(before, counts, preferred_element_type=F32)
    places = []
    for k in range(2):
        slot = jnp.sum(jnp.where(match[k], earlier, 0.0), axis=1, keepdims=True)
        places.append(ids[:, k : k + 1] * cap + slot.astype(jnp.int32))
    target = lax.broadcasted_iota(jnp.int32, (tok_rows, total), 1)
    hit = [places[k] == target for k in range(2)]
    wts = wts_ref[...]
    mix[...] = jnp.where(hit[0], wts[:, 0:1], 0.0) + jnp.where(hit[1], wts[:, 1:2], 0.0)
    spread = (hit[0].astype(F32) + hit[1].astype(F32)).astype(BF16)
    first_dims = (((0,), (0,)), ((), ()))
    my_columns = tok_ref[:, pl.ds(pl.multiple_of(me * width, 128), width)]
    placed = lax.dot_general(spread, my_columns, first_dims, preferred_element_type=F32)
    outgoing[...] = placed.astype(BF16).reshape(experts, cap, width)

    pl.semaphore_wait(barrier, experts + 1)

    def remote(src, dst, send, recv, **device):
        return pltpu.make_async_remote_copy(
            src_ref=src, dst_ref=dst, send_sem=send, recv_sem=recv,
            device_id=device, device_id_type=MESH,
        )

    sent = []

    def go(copy):
        copy.start()
        sent.append(copy)
        return copy

    z_copies = [
        go(remote(outgoing.at[others[d]], rows.at[me, z], z_send.at[d], z_recv.at[d], expert=others[d]))
        for d in range(1, experts)
    ]

    wide = lax.broadcasted_iota(jnp.int32, (tok_rows, 128), 1)
    own_hit = [(places[k] - z * cap == wide) & (wide < cap) for k in range(2)]
    own_spread = (own_hit[0].astype(F32) + own_hit[1].astype(F32)).astype(BF16)
    for q in range(PARTS):
        own = lax.dot_general(
            own_spread, tok_ref[:, q * width : (q + 1) * width], first_dims, preferred_element_type=F32
        )
        rows[q, z] = own[:cap].astype(BF16)

    c_copies, x_copies, d_copies = [], [], []
    for d in range(1, experts):
        source = lax.rem(z + experts - d, experts)
        z_copies[d - 1].wait_recv()
        block = rows.at[me, source]
        x_copies.append(go(remote(block, block, x_send.at[d], x_recv.at[d], etp=x_peer)))
        c_copies.append(go(remote(block, block, c_send.at[d], c_recv.at[d], etp=core_peer)))
    for d in range(1, experts):
        source = lax.rem(z + experts - d, experts)
        x_copies[d - 1].wait_recv()
        block = rows.at[x_peer, source]
        d_copies.append(go(remote(block, block, d_send.at[d], d_recv.at[d], etp=core_peer)))
    for copy in weight_copies[: 2 * PARTS]:
        copy.wait()
    for d in range(1, experts):
        c_copies[d - 1].wait_recv()
        d_copies[d - 1].wait_recv()

    @pl.loop(0, units // TILE)
    def _(n):
        cols = pl.ds(pl.multiple_of(n * TILE, TILE), TILE)
        gate_act = jnp.zeros((total, TILE), F32)
        up_act = jnp.zeros((total, TILE), F32)
        for q in range(PARTS):
            block = rows[q].reshape(total, width)
            at = slice(q * width, (q + 1) * width)
            gate_act += jnp.dot(block, gate[at, cols], preferred_element_type=F32)
            up_act += jnp.dot(block, up[at, cols], preferred_element_type=F32)
        hidden[:, cols] = (gate_act / (1.0 + jnp.exp(-gate_act)) * up_act).astype(BF16)

    for copy in weight_copies[2 * PARTS :]:
        copy.wait()

    def project(q, target_ref):
        @pl.loop(0, width // TILE)
        def _(n):
            start = pl.multiple_of(n * TILE, TILE)
            cols = pl.ds(pl.multiple_of(q * width + n * TILE, TILE), TILE)
            value = jnp.dot(hidden[...], down[:, cols], preferred_element_type=F32)
            target_ref[:, :, pl.ds(start, TILE)] = value.reshape(experts, cap, TILE).astype(target_ref.dtype)

    project(diagonal, core_out.at[0])
    first = go(remote(core_out.at[0], core_in.at[0], pc_send.at[0], pc_recv.at[0], etp=core_peer))
    project(x_peer, far_sum)
    first.wait_recv()
    px = []
    order = [others[d] for d in range(1, experts)] + [z]
    for i, block in enumerate(order):
        x_out[block] = (far_sum[block] + core_in[0, block].astype(F32)).astype(BF16)
        px.append(go(remote(x_out.at[block], x_in.at[block], px_send.at[i], px_recv.at[i], etp=x_peer)))
    project(core_peer, core_out.at[1])
    second = go(remote(core_out.at[1], core_in.at[1], pc_send.at[1], pc_recv.at[1], etp=core_peer))
    project(me, own_sum)
    second.wait_recv()

    pz = []
    for i, block in enumerate(order):
        px[i].wait_recv()
        value = own_sum[block] + core_in[1, block].astype(F32) + x_in[block].astype(F32)
        if i < experts - 1:
            z_out[block] = value.astype(BF16)
            pz.append(go(remote(z_out.at[block], returned.at[z], pz_send.at[i], pz_recv.at[i], expert=block)))
        else:
            returned[z] = value.astype(BF16)
    for copy in pz:
        copy.wait_recv()

    back = returned[...].reshape(total, width)
    rest = mix[...]
    result = jnp.zeros((tok_rows, width), F32)
    for _ in range(3):
        piece = rest.astype(BF16)
        rest = rest - piece.astype(F32)
        result += jnp.dot(piece, back, preferred_element_type=F32)
    out_ref[...] = result.astype(BF16)
    for copy in sent:
        copy.wait_send()


def fused_body(tokens, expert_ids, route_weights, w_gate, w_up, w_down):
    experts = lax.axis_size("expert")
    tok_rows, model_width = tokens.shape
    cap = tok_rows * 5 // 8
    width = model_width // PARTS
    units = w_gate.shape[2]
    vmem = pl.BlockSpec(memory_space=pltpu.VMEM)
    hbm = pl.BlockSpec(memory_space=pl.ANY)
    blocks = (experts, cap, width)
    flops = 2 * 3 * experts * cap * model_width * units
    dma = pltpu.SemaphoreType.DMA
    return pl.pallas_call(
        functools.partial(layer_kernel, experts),
        out_shape=jax.ShapeDtypeStruct((tok_rows, width), BF16),
        in_specs=[vmem, vmem, vmem, hbm, hbm, hbm],
        out_specs=vmem,
        scratch_shapes=[
            pltpu.VMEM((model_width, units), BF16),
            pltpu.VMEM((model_width, units), BF16),
            pltpu.VMEM((units, model_width), BF16),
            pltpu.VMEM((PARTS,) + blocks, BF16),
            pltpu.VMEM(blocks, BF16),
            pltpu.VMEM((experts * cap, units), BF16),
            pltpu.VMEM((tok_rows, experts * cap), F32),
            pltpu.VMEM((2,) + blocks, BF16),
            pltpu.VMEM((2,) + blocks, BF16),
            pltpu.VMEM(blocks, F32),
            pltpu.VMEM(blocks, F32),
            pltpu.VMEM(blocks, BF16),
            pltpu.VMEM(blocks, BF16),
            pltpu.VMEM(blocks, BF16),
            pltpu.VMEM(blocks, BF16),
            dma((3, PARTS)),
        ]
        + [dma((experts,))] * 8
        + [dma((2,))] * 2
        + [dma((experts,))] * 4,
        compiler_params=pltpu.CompilerParams(
            collective_id=0, has_side_effects=True, vmem_limit_bytes=60 * 2**20
        ),
        cost_estimate=pl.CostEstimate(
            flops=flops, bytes_accessed=3 * model_width * units * 2, transcendentals=experts * cap * units
        ),
    )(expert_ids, route_weights, tokens, w_gate, w_up, w_down)


def solution(mesh):
    placed = (
        P(("groups", "expert"), None),
        P(("groups", "expert"), None),
        P(("groups", "expert"), None),
        P("expert", None, "etp"),
        P("expert", None, "etp"),
        P("expert", "etp", None),
    )
    body = fused_body if mesh.shape["etp"] == PARTS else wide_body
    return jax.shard_map(
        body, mesh=mesh, in_specs=placed, out_specs=P(("groups", "expert"), "etp"), check_vma=False
    )
```

time: 148 us -> 60.4 us (0.41)
  Pallas kernels: 0 us -> 55.5 us
  blocking collectives: 51.5 us -> 0 us
  waiting for transfers between devices: 43.5 us -> 0 us
  matrix products: 28.2 us -> 0 us
  between operations: 13.5 us -> 0.01 us
  starting transfers between devices: 4.62 us -> 0 us
  other arithmetic: 3.14 us -> 0 us
    pallas_call x0 -> x1, Pallas kernels: none -> 55.5 us  [fused_body(): pl.pallas_call(functools.partial(layer_kernel, experts), out_shape=jax.Sh...]
    all_to_all x1 -> x0, blocking collectives: 51.5 us -> none  [body(): lax.all_to_all(outgoing, 'expert', split_axis=0, concat_axis=0, tiled=True)]
    reduce_scatter x1 -> x0, waiting for transfers between devices: 29.9 us -> none  [body(): lax.psum_scatter(partial_value, 'etp', scatter_dimension=2, tiled=True)]
    dot_general x3 -> x0, matrix products: 28.2 us -> none  [the longest x1 18.7 us: body(): jnp.dot(hidden, down_local, preferred_element_type=jnp.float32)]
    all_to_all x1 -> x0, waiting for transfers between devices: 13.5 us -> none  [body(): lax.all_to_all(expert_out, 'expert', split_axis=0, concat_axis=0, tiled=T...]
    all_to_all x1 -> x0, starting transfers between devices: 4.62 us -> none  [body(): lax.all_to_all(expert_out, 'expert', split_axis=0, concat_axis=0, tiled=T...]
    unnamed x6 -> x3, local copies, waits for them, and re-layouts: 0.98 us -> 4.43 us
    reduce_sum x3 -> x0, other arithmetic: 1.77 us -> none  [the longest x1 1.69 us: body(): combined = jnp.sum(weighted.reshape(tok_rows, 2, slice_width), axis=1)]
  transfers between devices with their start and end apart: 2 -> 0, of which waited for: 2 -> 0; matrix products, arithmetic and copies ran while one was open for 0% -> 0% of each run, Pallas kernels for 0% -> 0%
where the time goes in v1:
time: 60.4 us; the launch traced here: 60 us
  Pallas kernels  55.5 us (92%)
  local copies, waits for them, and re-layouts  4.43 us (7%)
    pallas_call x1, Pallas kernels, fused_body(): pl.pallas_call(functools.partial(layer_kernel, experts), out_shape=jax.Sh...  55.5 us
    unnamed x3, local copies, waits for them, and re-layouts  4.43 us

profile of v1, /device:TPU:0, one launch (start us, length us, event | category | flops | bytes accessed | tf_op | source)
XLA Modules:
  0.0 60.0 jit_solution(3092637207409061184)
XLA Ops:
  0.0 1.4 %copy.7.ids_ref = s32[128,2]{1,0:T(8,128)} copy(s32[128,2]{0,1:T(2,128)} %param.7) | data formatting | bytes 2048 | tf_op args[1]
  1.4 1.4 %copy.8.wts_ref = f32[128,2]{1,0:T(8,128)} copy(f32[128,2]{0,1:T(2,128)} %param.8) | data formatting | bytes 2048 | tf_op args[2]
  2.8 55.5 %shard_map.64 = bf16[128,768]{1,0:T(8,128)(2,1)} custom-call(s32[128,2]{1,0:T(8,128)} %copy.7.ids_ref, f32[128,2]{1,0:T(8,128)} %copy.8.wts_ref, bf16[128,3072]{1,0:T(8,128)(2,1)} %tok_ref.1, bf16[1,3072,2048]{2,1,0:T(8,128)(2,1)} %gate_hbm.1, bf16[1,3072,2048]{2,1,0:T(8,128)(2,1)} %up_hbm.1, bf16[1,2048,3072]{2,1,0:T(8,128)(2,1)} %down_hbm.1), custom_call_target="tpu_custom_call" | custom-call | flops 12079595520 | bytes 37748736 | tf_op jit(solution)/shard_map/pallas_call | solution.py:242
  58.3 1.6 %copy.10 = bf16[128,768]{1,0:T(8,128)(2,1)} copy(bf16[128,768]{1,0:T(8,128)(2,1)} %shard_map.64) | data formatting | bytes 393216

commit v2 on v1

--- a/solution.py
+++ b/solution.py
@@ -11,6 +11,7 @@
 F32 = jnp.float32
 BF16 = jnp.bfloat16
 TILE = 256
+WIDE = 1024
 PARTS = 4
 
 
@@ -58,11 +59,11 @@
 
 def layer_kernel(
     experts,
-    ids_ref, wts_ref, tok_ref, gate_hbm, up_hbm, down_hbm,
+    ids_ref, wts_ref, tok_hbm, gate_hbm, up_hbm, down_hbm,
     out_ref,
-    gate, up, down, rows, outgoing, hidden, mix,
+    tok_ref, gate, up, down, rows, outgoing, gate_sum, up_sum, hidden, mix,
     core_out, core_in, far_sum, own_sum, x_out, x_in, z_out, returned,
-    w_sem, z_send, z_recv, c_send, c_recv, x_send, x_recv, d_send, d_recv,
+    tok_sem, w_sem, z_send, z_recv, c_send, c_recv, x_send, x_recv, d_send, d_recv,
     pc_send, pc_recv, px_send, px_recv, pz_send, pz_recv,
 ):
     me = lax.axis_index("etp")
@@ -78,18 +79,8 @@
     total = experts * cap
     units = hidden.shape[1]
 
-    in_chunk = gate.shape[0] // PARTS
-    down_chunk = down.shape[0] // PARTS
-    weight_copies = []
-    for part in range(PARTS):
-        at = slice(part * in_chunk, (part + 1) * in_chunk)
-        weight_copies.append(pltpu.make_async_copy(gate_hbm.at[0, at], gate.at[at], w_sem.at[0, part]))
-        weight_copies.append(pltpu.make_async_copy(up_hbm.at[0, at], up.at[at], w_sem.at[1, part]))
-    for part in range(PARTS):
-        at = slice(part * down_chunk, (part + 1) * down_chunk)
-        weight_copies.append(pltpu.make_async_copy(down_hbm.at[0, at], down.at[at], w_sem.at[2, part]))
-    for copy in weight_copies:
-        copy.start()
+    tok_copy = pltpu.make_async_copy(tok_hbm, tok_ref, tok_sem)
+    tok_copy.start()
 
     barrier = pltpu.get_barrier_semaphore()
     others = [lax.rem(z + d, experts) for d in range(experts)]
@@ -99,25 +90,36 @@
         pl.semaphore_signal(barrier, inc=1, device_id={"etp": peer}, device_id_type=MESH)
 
     ids = ids_ref[...]
-    lane = lax.broadcasted_iota(jnp.int32, (tok_rows, 128), 1)
-    match = [ids[:, k : k + 1] == lane for k in range(2)]
+    wts = wts_ref[...]
+    label = lax.broadcasted_iota(jnp.int32, (2 * PARTS if experts <= 2 * PARTS else experts, tok_rows), 0)
+    match = [ids[k : k + 1] == label for k in range(2)]
     counts = (match[0].astype(F32) + match[1].astype(F32)).astype(BF16)
     row_at = lax.broadcasted_iota(jnp.int32, (tok_rows, tok_rows), 0)
     col_at = lax.broadcasted_iota(jnp.int32, (tok_rows, tok_rows), 1)
-    before = (col_at < row_at).astype(F32).astype(BF16)
-    earlier = jnp.dot(before, counts, preferred_element_type=F32)
+    before = (row_at < col_at).astype(F32).astype(BF16)
+    earlier = jnp.dot(counts, before, preferred_element_type=F32)
     places = []
     for k in range(2):
-        slot = jnp.sum(jnp.where(match[k], earlier, 0.0), axis=1, keepdims=True)
-        places.append(ids[:, k : k + 1] * cap + slot.astype(jnp.int32))
-    target = lax.broadcasted_iota(jnp.int32, (tok_rows, total), 1)
+        slot = jnp.sum(jnp.where(match[k], earlier, 0.0), axis=0, keepdims=True)
+        places.append(ids[k : k + 1] * cap + slot.astype(jnp.int32))
+    target = lax.broadcasted_iota(jnp.int32, (total, tok_rows), 0)
     hit = [places[k] == target for k in range(2)]
-    wts = wts_ref[...]
-    mix[...] = jnp.where(hit[0], wts[:, 0:1], 0.0) + jnp.where(hit[1], wts[:, 1:2], 0.0)
     spread = (hit[0].astype(F32) + hit[1].astype(F32)).astype(BF16)
-    first_dims = (((0,), (0,)), ((), ()))
+    tok_copy.wait()
+
+    down_chunk = down.shape[0] // PARTS
+    gate_copies, down_copies = [], []
+    for i, q in enumerate((me, core_peer, x_peer, diagonal)):
+        at = pl.ds(pl.multiple_of(q * width, width), width)
+        gate_copies.append(pltpu.make_async_copy(gate_hbm.at[0, at], gate.at[at], w_sem.at[0, i]))
+        gate_copies.append(pltpu.make_async_copy(up_hbm.at[0, at], up.at[at], w_sem.at[1, i]))
+    for part in range(PARTS):
+        at = slice(part * down_chunk, (part + 1) * down_chunk)
+        down_copies.append(pltpu.make_async_copy(down_hbm.at[0, at], down.at[at], w_sem.at[2, part]))
+    for copy in gate_copies:
+        copy.start()
     my_columns = tok_ref[:, pl.ds(pl.multiple_of(me * width, 128), width)]
-    placed = lax.dot_general(spread, my_columns, first_dims, preferred_element_type=F32)
+    placed = jnp.dot(spread, my_columns, preferred_element_type=F32)
     outgoing[...] = placed.astype(BF16).reshape(experts, cap, width)
 
     pl.semaphore_wait(barrier, experts + 1)
@@ -136,50 +138,89 @@
         return copy
 
     z_copies = [
-        go(remote(outgoing.at[others[d]], rows.at[me, z], z_send.at[d], z_recv.at[d], expert=others[d]))
+        go(remote(outgoing.at[others[d]], rows.at[me, d], z_send.at[d], z_recv.at[d], expert=others[d]))
         for d in range(1, experts)
     ]
 
-    wide = lax.broadcasted_iota(jnp.int32, (tok_rows, 128), 1)
-    own_hit = [(places[k] - z * cap == wide) & (wide < cap) for k in range(2)]
+    slot_at = lax.broadcasted_iota(jnp.int32, (cap, tok_rows), 0) + z * cap
+    own_hit = [places[k] == slot_at for k in range(2)]
     own_spread = (own_hit[0].astype(F32) + own_hit[1].astype(F32)).astype(BF16)
     for q in range(PARTS):
-        own = lax.dot_general(
-            own_spread, tok_ref[:, q * width : (q + 1) * width], first_dims, preferred_element_type=F32
-        )
-        rows[q, z] = own[:cap].astype(BF16)
+        own = jnp.dot(own_spread, tok_ref[:, q * width : (q + 1) * width], preferred_element_type=F32)
+        rows[q, 0] = own.astype(BF16)
+
+    rest = jnp.where(hit[0], wts[0:1], 0.0) + jnp.where(hit[1], wts[1:2], 0.0)
+    diagonal_ones = (row_at == col_at).astype(F32).astype(BF16)
+    for i in range(3):
+        piece = rest.astype(BF16)
+        rest = rest - piece.astype(F32)
+        turned = lax.dot_general(diagonal_ones, piece, (((1,), (1,)), ((), ())), preferred_element_type=F32)
+        mix[i] = turned.astype(BF16)
+
+    def own_part(low, high):
+        @pl.loop(low, high)
+        def _(n):
+            cols = pl.ds(pl.multiple_of(n * WIDE, WIDE), WIDE)
+            gate_act = jnp.zeros((cap, WIDE), F32)
+            up_act = jnp.zeros((cap, WIDE), F32)
+            for q in range(PARTS):
+                at = slice(q * width, (q + 1) * width)
+                gate_act += jnp.dot(rows[q, 0], gate[at, cols], preferred_element_type=F32)
+                up_act += jnp.dot(rows[q, 0], up[at, cols], preferred_element_type=F32)
+            hidden[:cap, cols] = (gate_act / (1.0 + jnp.exp(-gate_act)) * up_act).astype(BF16)
+
+    rest_rows = total - cap
+
+    def multiply(q, is_first, is_last):
+        @pl.loop(0, units // WIDE)
+        def _(n):
+            cols = pl.ds(pl.multiple_of(n * WIDE, WIDE), WIDE)
+            at = pl.ds(pl.multiple_of(q * width, width), width)
+            block = rows[q, 1:].reshape(rest_rows, width)
+            gate_act = jnp.dot(block, gate[at, cols], preferred_element_type=F32)
+            up_act = jnp.dot(block, up[at, cols], preferred_element_type=F32)
+            if not is_first:
+                gate_act += gate_sum[:, cols]
+                up_act += up_sum[:, cols]
+            if is_last:
+                hidden[cap:, cols] = (gate_act / (1.0 + jnp.exp(-gate_act)) * up_act).astype(BF16)
+            else:
+                gate_sum[:, cols] = gate_act
+                up_sum[:, cols] = up_act
 
     c_copies, x_copies, d_copies = [], [], []
     for d in range(1, experts):
-        source = lax.rem(z + experts - d, experts)
         z_copies[d - 1].wait_recv()
-        block = rows.at[me, source]
+        block = rows.at[me, d]
         x_copies.append(go(remote(block, block, x_send.at[d], x_recv.at[d], etp=x_peer)))
         c_copies.append(go(remote(block, block, c_send.at[d], c_recv.at[d], etp=core_peer)))
-    for d in range(1, experts):
-        source = lax.rem(z + experts - d, experts)
+        if d == 1:
+            for copy in gate_copies:
+                copy.wait()
+            for copy in down_copies:
+                copy.start()
+            own_part(0, units // WIDE // 2)
+        if d == 2:
+            own_part(units // WIDE // 2, units // WIDE)
+
+    def pass_on(d):
         x_copies[d - 1].wait_recv()
-        block = rows.at[x_peer, source]
+        block = rows.at[x_peer, d]
         d_copies.append(go(remote(block, block, d_send.at[d], d_recv.at[d], etp=core_peer)))
-    for copy in weight_copies[: 2 * PARTS]:
-        copy.wait()
-    for d in range(1, experts):
-        c_copies[d - 1].wait_recv()
-        d_copies[d - 1].wait_recv()
-
-    @pl.loop(0, units // TILE)
-    def _(n):
-        cols = pl.ds(pl.multiple_of(n * TILE, TILE), TILE)
-        gate_act = jnp.zeros((total, TILE), F32)
-        up_act = jnp.zeros((total, TILE), F32)
-        for q in range(PARTS):
-            block = rows[q].reshape(total, width)
-            at = slice(q * width, (q + 1) * width)
-            gate_act += jnp.dot(block, gate[at, cols], preferred_element_type=F32)
-            up_act += jnp.dot(block, up[at, cols], preferred_element_type=F32)
-        hidden[:, cols] = (gate_act / (1.0 + jnp.exp(-gate_act)) * up_act).astype(BF16)
-
-    for copy in weight_copies[2 * PARTS :]:
+
+    multiply(me, True, False)
+    for d in range(1, experts - 1):
+        pass_on(d)
+    for copy in c_copies:
+        copy.wait_recv()
+    multiply(core_peer, False, False)
+    pass_on(experts - 1)
+    multiply(x_peer, False, False)
+    for copy in d_copies:
+        copy.wait_recv()
+    multiply(diagonal, False, True)
+
+    for copy in down_copies:
         copy.wait()
 
     def project(q, target_ref):
@@ -195,7 +236,7 @@
     project(x_peer, far_sum)
     first.wait_recv()
     px = []
-    order = [others[d] for d in range(1, experts)] + [z]
+    order = list(range(1, experts)) + [0]
     for i, block in enumerate(order):
         x_out[block] = (far_sum[block] + core_in[0, block].astype(F32)).astype(BF16)
         px.append(go(remote(x_out.at[block], x_in.at[block], px_send.at[i], px_recv.at[i], etp=x_peer)))
@@ -210,20 +251,17 @@
         value = own_sum[block] + core_in[1, block].astype(F32) + x_in[block].astype(F32)
         if i < experts - 1:
             z_out[block] = value.astype(BF16)
-            pz.append(go(remote(z_out.at[block], returned.at[z], pz_send.at[i], pz_recv.at[i], expert=block)))
+            pz.append(go(remote(z_out.at[block], returned.at[z], pz_send.at[i], pz_recv.at[i], expert=lax.rem(z + experts - block, experts))))
         else:
             returned[z] = value.astype(BF16)
     for copy in pz:
         copy.wait_recv()
 
     back = returned[...].reshape(total, width)
-    rest = mix[...]
     result = jnp.zeros((tok_rows, width), F32)
-    for _ in range(3):
-        piece = rest.astype(BF16)
-        rest = rest - piece.astype(F32)
-        result += jnp.dot(piece, back, preferred_element_type=F32)
-    out_ref[...] = result.astype(BF16)
+    for i in range(3):
+        result += jnp.dot(mix[i], back, preferred_element_type=F32)
+    out_ref[...] = result
     for copy in sent:
         copy.wait_send()
 
@@ -241,17 +279,20 @@
     dma = pltpu.SemaphoreType.DMA
     return pl.pallas_call(
         functools.partial(layer_kernel, experts),
-        out_shape=jax.ShapeDtypeStruct((tok_rows, width), BF16),
-        in_specs=[vmem, vmem, vmem, hbm, hbm, hbm],
+        out_shape=jax.ShapeDtypeStruct((tok_rows, width), F32),
+        in_specs=[vmem, vmem, hbm, hbm, hbm, hbm],
         out_specs=vmem,
         scratch_shapes=[
+            pltpu.VMEM((tok_rows, model_width), BF16),
             pltpu.VMEM((model_width, units), BF16),
             pltpu.VMEM((model_width, units), BF16),
             pltpu.VMEM((units, model_width), BF16),
             pltpu.VMEM((PARTS,) + blocks, BF16),
             pltpu.VMEM(blocks, BF16),
+            pltpu.VMEM(((experts - 1) * cap, units), F32),
+            pltpu.VMEM(((experts - 1) * cap, units), F32),
             pltpu.VMEM((experts * cap, units), BF16),
-            pltpu.VMEM((tok_rows, experts * cap), F32),
+            pltpu.VMEM((3, tok_rows, experts * cap), BF16),
             pltpu.VMEM((2,) + blocks, BF16),
             pltpu.VMEM((2,) + blocks, BF16),
             pltpu.VMEM(blocks, F32),
@@ -260,6 +301,7 @@
             pltpu.VMEM(blocks, BF16),
             pltpu.VMEM(blocks, BF16),
             pltpu.VMEM(blocks, BF16),
+            dma,
             dma((3, PARTS)),
         ]
         + [dma((experts,))] * 8
@@ -271,7 +313,7 @@
         cost_estimate=pl.CostEstimate(
             flops=flops, bytes_accessed=3 * model_width * units * 2, transcendentals=experts * cap * units
         ),
-    )(expert_ids, route_weights, tokens, w_gate, w_up, w_down)
+    )(expert_ids.T, route_weights.T, tokens, w_gate, w_up, w_down).astype(BF16)
 
 
 def solution(mesh):

time: 60.4 us -> 52.8 us (0.87)
  Pallas kernels: 55.5 us -> 50.9 us
  local copies, waits for them, and re-layouts: 4.43 us -> 0 us
  other arithmetic: 0 us -> 1.69 us
    pallas_call x1, Pallas kernels: 55.5 us -> 50.9 us  [fused_body(): pl.pallas_call(functools.partial(layer_kernel, experts), out_shape=jax.Sh...]
    unnamed x3 -> x0, local copies, waits for them, and re-layouts: 4.43 us -> none
    convert_element_type x0 -> x1, other arithmetic: none -> 1.69 us  [fused_body(): return pl.pallas_call(functools.partial(layer_kernel, experts), out_shape...]
where the time goes in v2:
time: 52.8 us; the launch traced here: 52.6 us
  Pallas kernels  50.9 us (96%)
  other arithmetic  1.69 us (3%)
    pallas_call x1, Pallas kernels, fused_body(): pl.pallas_call(functools.partial(layer_kernel, experts), out_shape=jax.Sh...  50.9 us
    convert_element_type x1, other arithmetic, fused_body(): return pl.pallas_call(functools.partial(layer_kernel, experts), out_shape...  1.69 us

profile of v2, /device:TPU:0, one launch (start us, length us, event | category | flops | bytes accessed | tf_op | source)
XLA Modules:
  0.0 52.6 jit_solution(9047585297352882497)
XLA Ops:
  0.0 50.9 %shard_map.64 = f32[128,768]{1,0:T(8,128)} custom-call(s32[2,128]{1,0:T(2,128)} %bitcast.2, f32[2,128]{1,0:T(2,128)} %bitcast.3, bf16[128,3072]{1,0:T(8,128)(2,1)} %tok_hbm.1, bf16[1,3072,2048]{2,1,0:T(8,128)(2,1)} %gate_hbm.1, bf16[1,3072,2048]{2,1,0:T(8,128)(2,1)} %up_hbm.1, bf16[1,2048,3072]{2,1,0:T(8,128)(2,1)} %down_hbm.1), custom_call_target="tpu_custom_call" | custom-call | flops 12079595520 | bytes 37748736 | tf_op jit(solution)/shard_map/pallas_call | solution.py:280
  50.9 1.7 %convert_element_type.3 = bf16[128,768]{1,0:T(8,128)(2,1)} convert(f32[128,768]{1,0:T(8,128)} %shard_map.64) | non-fusion elementwise | flops 98304 | bytes 589824 | tf_op jit(solution)/shard_map/convert_element_type | solution.py:316

commit v3 on v2

--- a/solution.py
+++ b/solution.py
@@ -236,7 +236,8 @@
     project(x_peer, far_sum)
     first.wait_recv()
     px = []
-    order = list(range(1, experts)) + [0]
+    middle = experts // 2
+    order = [middle] + [d for d in range(1, experts) if d != middle] + [0]
     for i, block in enumerate(order):
         x_out[block] = (far_sum[block] + core_in[0, block].astype(F32)).astype(BF16)
         px.append(go(remote(x_out.at[block], x_in.at[block], px_send.at[i], px_recv.at[i], etp=x_peer)))

time: 52.8 us -> 50.5 us (0.956)
  Pallas kernels: 50.9 us -> 48.5 us
    pallas_call x1, Pallas kernels: 50.9 us -> 48.5 us  [fused_body(): pl.pallas_call(functools.partial(layer_kernel, experts), out_shape=jax.Sh...]
where the time goes in v3:
time: 50.5 us; the launch traced here: 50.2 us
  Pallas kernels  48.5 us (96%)
  other arithmetic  1.69 us (3%)
    pallas_call x1, Pallas kernels, fused_body(): pl.pallas_call(functools.partial(layer_kernel, experts), out_shape=jax.Sh...  48.5 us
    convert_element_type x1, other arithmetic, fused_body(): return pl.pallas_call(functools.partial(layer_kernel, experts), out_shape...  1.69 us

profile of v3, /device:TPU:0, one launch (start us, length us, event | category | flops | bytes accessed | tf_op | source)
XLA Modules:
  0.0 50.2 jit_solution(8336080138608400919)
XLA Ops:
  0.0 48.5 %shard_map.64 = f32[128,768]{1,0:T(8,128)} custom-call(s32[2,128]{1,0:T(2,128)} %bitcast.2, f32[2,128]{1,0:T(2,128)} %bitcast.3, bf16[128,3072]{1,0:T(8,128)(2,1)} %tok_hbm.1, bf16[1,3072,2048]{2,1,0:T(8,128)(2,1)} %gate_hbm.1, bf16[1,3072,2048]{2,1,0:T(8,128)(2,1)} %up_hbm.1, bf16[1,2048,3072]{2,1,0:T(8,128)(2,1)} %down_hbm.1), custom_call_target="tpu_custom_call" | custom-call | flops 12079595520 | bytes 37748736 | tf_op jit(solution)/shard_map/pallas_call | solution.py:281
  48.5 1.7 %convert_element_type.3 = bf16[128,768]{1,0:T(8,128)(2,1)} convert(f32[128,768]{1,0:T(8,128)} %shard_map.64) | non-fusion elementwise | flops 98304 | bytes 589824 | tf_op jit(solution)/shard_map/convert_element_type | solution.py:317
